TPU v7x, 32 devices: a whole 2x2x4 slice. The times are simulated.
32 devices in a mesh: groups: 2 (over y), cells: 4 (over z), role: 2 (over x), sub: 2 (over core).
Axes of the slice: x: 2, y: 2, z: 4, core: 2. Of those that a mesh axis runs over, the one named last changes fastest.
Arguments:
- tracers: float32 [16, 80, 4096], P('sub', None, ('groups', 'cells', 'role')), parts along dimension 2, may hold values from -6 to 6
- layer_count: int32 [4096], P(('groups', 'cells', 'role')), parts along dimension 0, may hold values from 40 to 80
- neighbor: int32 [6, 4096], P(None, ('groups', 'cells', 'role')), parts along dimension 1, may hold values from 0 to 511, as said below
- halo_cells: int32 [2, 2048], P(None, ('groups', 'cells', 'role')), parts along dimension 1, may hold values from 0 to 255, as said below
- transport: float32 [80, 24576], P('sub', ('groups', 'cells', 'role')), parts along dimension 1, may hold values from -0.4 to 0.4
- edge_diff: float32 [80, 24576], P('sub', ('groups', 'cells', 'role')), parts along dimension 1, may hold values from 0.02 to 0.08
- record_dest: int32 [24576], P(('groups', 'cells', 'role')), parts along dimension 0, may hold values from 0 to 7, as said below
- record_slot: int32 [24576], P(('groups', 'cells', 'role')), parts along dimension 0, may hold values from 0 to 1535, as said below
- vert_diff: float32 [80, 4096], P(None, ('groups', 'cells', 'role')), parts along dimension 1, may hold values from 0.02 to 0.24
- half_sat: float32 [16], replicated, may hold values from 0.1 to 2
- stoich: float32 [16, 16], replicated, may hold values from -1.5 to 1.5
Outputs:
- tracers_next: float32 [16, 80, 4096], P('sub', None, ('groups', 'cells', 'role')), parts along dimension 2
There are 2 independent parts, one for each index of `groups`. A program takes and returns all parts, laid end to end along the dimension named above; an argument that names none is the same for every part. Nothing has to cross between parts.
Inputs may be any that keep to these rules, and one draw needn't show every extreme that they name: `neighbor`: the cells form a hexagonal mesh of rows of 128 cells, periodic in both directions, 2 rows to a block; the neighbour relation is symmetric. An index below 256 is a cell of the same block, the others address the adjacent blocks' halo_cells lists as the steps say. `halo_cells`: for each block, two lists of 128 distinct local cells: first the cells that the previous block reads, then those that the next block reads. `record_dest`: among the records of one device, no block is named more than 384 times, and in every draw each device names some block exactly 384 times; every block is named by 1536 records in all. `record_slot`: every pair of a block and a slot is named by exactly one record.
All inputs are finite; a program needn't handle non-finite values.
Results may differ from a plain program's by a relative error of at most 0.00005.
Values sent between devices are 32-bit elements; how exact they have to be, the bound alone decides.
A program may use at most 128 MiB of HBM per device.

v0:
```python
import jax
import jax.numpy as jnp
from jax import lax
from jax.sharding import PartitionSpec as P

LIMIT_PAD = 1.5
REACT_RATE = 0.5


def extended_2(block, sides, width):
    for axis, dim in sides:
        count = lax.axis_size(axis)
        forward = [(i, i + 1) for i in range(count - 1)]
        forward.append((count - 1, 0))
        backward = [(target, source) for source, target in forward]
        low = lax.ppermute(
            lax.slice_in_dim(block, block.shape[dim] - width, None, axis=dim), axis, forward
        )
        high = lax.ppermute(lax.slice_in_dim(block, 0, width, axis=dim), axis, backward)
        block = jnp.concatenate([low, block, high], axis=dim)
    return block


def edge_terms(field, beyond, open_mask, flow, kappa):
    upwind = open_mask * (jnp.maximum(flow, 0.0) * field + jnp.minimum(flow, 0.0) * beyond)
    antidiff = open_mask * (0.5 * flow * (field + beyond)) - upwind
    diffuse = open_mask * kappa * (beyond - field)
    return (upwind, antidiff, diffuse)


def rim_rows(rows, halo_cells):
    picked = rows[halo_cells]
    return picked


def body(
    tracers,
    layer_count,
    neighbor,
    halo_cells,
    transport,
    edge_diff,
    record_dest,
    record_slot,
    vert_diff,
    half_sat,
    stoich,
):
    tracer_count, layer_total, cell_count = tracers.shape
    flat_width = tracer_count * layer_total
    blocks = lax.axis_size(("cells", "role"))
    record_count = record_dest.shape[0]
    capacity = 2 * record_count // blocks
    matches = (record_dest[:, None] == jnp.arange(blocks, dtype=jnp.int32)[None, :]).astype(
        jnp.int32
    )
    order_in = jnp.sum(jnp.cumsum(matches, axis=0) * matches, axis=1) - 1
    target = record_dest * capacity + order_in
    payload = jnp.concatenate([transport, edge_diff], axis=0).T
    payload_cols = payload.shape[1]
    outgoing = jnp.zeros((blocks * capacity, payload_cols), jnp.float32).at[target].set(payload)
    labels = jnp.full((blocks * capacity,), record_count, jnp.int32).at[target].set(record_slot)
    arrived, arrived_slot = (
        lax.all_to_all(outgoing, ("cells", "role"), split_axis=0, concat_axis=0, tiled=True),
        lax.all_to_all(labels, ("cells", "role"), split_axis=0, concat_axis=0, tiled=True),
    )
    edge_table = (
        jnp.zeros((record_count, payload_cols), jnp.float32)
        .at[arrived_slot]
        .set(arrived, mode="drop")
    )
    edge_table = lax.all_gather(edge_table.reshape(record_count, 2, -1), "sub", axis=2, tiled=True)
    flow_edges = edge_table[:, 0, :].reshape(6, cell_count, layer_total)
    kappa_edges = edge_table[:, 1, :].reshape(6, cell_count, layer_total)
    wet_rows = (jnp.arange(layer_total, dtype=jnp.int32)[None, :] < layer_count[:, None]).astype(
        jnp.float32
    )
    wet_flat = jnp.tile(wet_rows, (1, tracer_count))
    field = tracers.transpose(2, 0, 1).reshape(cell_count, flat_width)
    stacked = jnp.concatenate([field, wet_rows], axis=1)
    cycle = extended_2(rim_rows(stacked, halo_cells), ((("cells", "role"), 0),), 1)
    extended = jnp.concatenate([stacked, cycle[0], cycle[3]], axis=0)
    total_abs = jnp.zeros_like(field)
    upper_bound = field
    lower_bound = field
    saved = []
    for slot_index in range(6):
        nb_cells = neighbor[slot_index]
        gathered = extended[nb_cells]
        beyond = gathered[:, :flat_width]
        far_wet = jnp.tile(gathered[:, flat_width:], (1, tracer_count))
        open_mask = wet_flat * far_wet
        flow_flat = jnp.tile(flow_edges[slot_index], (1, tracer_count))
        kappa_flat = jnp.tile(kappa_edges[slot_index], (1, tracer_count))
        upwind, antidiff, diffuse = edge_terms(field, beyond, open_mask, flow_flat, kappa_flat)
        total_abs = total_abs + jnp.abs(antidiff)
        candidate = jnp.where(open_mask > 0, beyond, field)
        upper_bound = jnp.maximum(upper_bound, candidate)
        lower_bound = jnp.minimum(lower_bound, candidate)
        saved.append((upwind, antidiff, diffuse))
    spread = upper_bound - lower_bound
    limiter_ratio = spread / (spread + total_abs + LIMIT_PAD)
    limit_cycle = extended_2(rim_rows(limiter_ratio, halo_cells), ((("cells", "role"), 0),), 1)
    limit_ext = jnp.concatenate([limiter_ratio, limit_cycle[0], limit_cycle[3]], axis=0)
    net_flux = jnp.zeros_like(field)
    for slot_index in range(6):
        upwind, antidiff, diffuse = saved[slot_index]
        bound = jnp.minimum(limiter_ratio, limit_ext[neighbor[slot_index]])
        net_flux = net_flux + (upwind + bound * antidiff - diffuse)
    advected = field - net_flux
    layer_pos = jnp.arange(layer_total, dtype=jnp.int32)
    next_wet = jnp.concatenate([wet_rows[:, 1:], jnp.zeros_like(wet_rows[:, :1])], axis=1)
    coupling = jnp.where(
        layer_pos[None, :] < layer_total - 1, vert_diff.T * wet_rows * next_wet, 0.0
    )
    coupling_flat = jnp.tile(coupling, (1, tracer_count))
    zero_col = jnp.zeros_like(advected[:, :1])
    upper_diff = jnp.concatenate([advected[:, 1:], zero_col], axis=1) - advected
    vertical = coupling_flat * upper_diff
    vertical_below = jnp.concatenate([zero_col, vertical[:, :-1]], axis=1)
    mixed_field = advected + vertical - vertical_below
    offset = lax.axis_index("sub") * tracer_count
    every = lax.all_gather(mixed_field, "sub", axis=1, tiled=True)
    sat_flat = jnp.repeat(half_sat, layer_total)
    uptake = every * every / (sat_flat[None, :] + every * every)
    own_rates = lax.dynamic_slice_in_dim(stoich, offset, tracer_count, 0)
    reaction = jnp.einsum(
        "ij,cjl->cil",
        own_rates,
        uptake.reshape(cell_count, -1, layer_total),
        precision=lax.Precision.HIGHEST,
    )
    reaction = reaction.reshape(cell_count, flat_width)
    sunlight = jnp.exp(-3.0 * jnp.arange(layer_total, dtype=jnp.float32) / layer_total)
    light_flat = jnp.tile(sunlight[None, :] * wet_rows, (1, tracer_count))
    result = mixed_field + REACT_RATE * light_flat * reaction
    return result.reshape(cell_count, tracer_count, layer_total).transpose(1, 2, 0)


def solution(mesh):
    in_specs = (
        P("sub", None, ("groups", "cells", "role")),
        P(("groups", "cells", "role")),
        P(None, ("groups", "cells", "role")),
        P(None, ("groups", "cells", "role")),
        P("sub", ("groups", "cells", "role")),
        P("sub", ("groups", "cells", "role")),
        P(("groups", "cells", "role")),
        P(("groups", "cells", "role")),
        P(None, ("groups", "cells", "role")),
        P(),
        P(),
    )
    out_specs = P("sub", None, ("groups", "cells", "role"))
    return jax.shard_map(body, mesh=mesh, in_specs=in_specs, out_specs=out_specs, check_vma=False)
```

profile of v0, /device:TPU:0, one launch (start us, length us, event | category | flops | bytes accessed | tf_op | source)
XLA Modules:
  0.0 192.7 jit_solution(18004431007526948883)
XLA Ops:
  6.5 1.3 copy.484
  8.8 1.1 gather_fusion
  10.8 2.9 %collective-permute-start = (f32[1,128,720]{2,1,0:T(8,128)}, f32[1,128,720]{2,1,0:T(8,128)S(1)}, u32[]{:S(2)}, u32[]{:S(2)}) collective-permute-start(f32[1,128,720]{2,1,0:T(8,128)} %get-tuple-element.29), channel_id=1, source_target_pairs={{0,2},{2,4},{4,6},{6,8},{8,10},{10,12},{12,14},{14,0},{1,3},{3,5},... | collective-permute-start | bytes 1105928 | tf_op jit(solution)/shard_map/ppermute | solution.py:16
  13.8 3.0 %collective-permute-start.1 = (f32[1,128,720]{2,1,0:T(8,128)}, f32[1,128,720]{2,1,0:T(8,128)}, u32[]{:S(2)}, u32[]{:S(2)}) collective-permute-start(f32[1,128,720]{2,1,0:T(8,128)} %get-tuple-element.30), channel_id=1, source_target_pairs={{2,0},{4,2},{6,4},{8,6},{10,8},{12,10},{14,12},{0,14},{3,1},{5,3},... | collective-permute-start | bytes 1105928 | tf_op jit(solution)/shard_map/ppermute | solution.py:19
  16.8 2.3 %reduce-window.6 = s32[8,12,128]{2,1,0:T(8,128)S(1)} reduce-window(s32[8,12,128]{2,1,0:T(8,128)S(1)} %fusion.32, s32[]{:T(128)} %constant.15.clone.1), window={size=1x1x128 pad=0_0x0_0x127_0}, to_apply=%region_0.0 | reduce-window | flops 1560576 | bytes 98308 | tf_op jit(solution)/shard_map/reduce-window
  19.7 6.9 %scatter_custom_fusion = s32[3072]{0:T(1024)} fusion(s32[1536]{0:T(1024)S(1)} %compare_select_fusion.1, s32[1536]{0:T(1024)} %param.18, s32[]{:T(128)} %constant.19.clone.1), kind=kCustom, calls=%fused_computation.112 | custom fusion | bytes 12800 | tf_op jit(solution)/shard_map/scatter | solution.py:62
  26.7 3.9 %all-to-all-start = ((s32[8,384,1]{1,2,0:T(1,128)}), s32[8,384,1]{1,2,0:T(1,128)}, u32[]{:S(2)}, u32[]{:S(2)}) async-start(s32[8,384,1]{1,2,0:T(1,128)} %bitcast.13), calls=%async_computation | async-start | bytes 24576 | tf_op jit(solution)/shard_map/all_to_all | solution.py:65
  32.6 4.9 %scatter_custom_fusion.1 = f32[3072,80]{1,0:T(8,128)S(1)} fusion(s32[1536]{0:T(1024)} %copy-done.27, f32[1536,80]{1,0:T(8,128)S(1)} %copy.400, f32[]{:T(128)} %constant.18.clone.1), kind=kCustom, calls=%fused_computation.27 | custom fusion | bytes 983552 | tf_op jit(solution)/shard_map/scatter | solution.py:61
  37.5 1.4 copy.401
  38.9 5.9 %all-to-all-start.1 = ((f32[8,384,80]{1,2,0:T(8,128)}), f32[8,384,80]{1,2,0:T(8,128)}, u32[]{:S(2)}, u32[]{:S(2)}) async-start(f32[8,384,80]{1,2,0:T(8,128)} %copy.401), calls=%async_computation.1 | async-start | bytes 1966080 | tf_op jit(solution)/shard_map/all_to_all | solution.py:64
  48.6 1.3 compare_select_fusion
  50.0 1.1 pad_maximum_fusion
  51.1 1.1 gather_fusion.1
  52.3 2.1 %gather_fusion.2 = f32[256,720]{1,0:T(8,128)} fusion(f32[512,720]{1,0:T(8,128)S(1)} %pad_maximum_fusion, s32[1024]{0:T(1024)} %pad_clamp_fusion.4), kind=kCustom, calls=%fused_computation.2 | custom fusion | bytes 1475584 | tf_op jit(solution)/shard_map/gather | solution.py:89
  55.4 2.1 %gather_fusion.3 = f32[256,720]{1,0:T(8,128)} fusion(f32[512,720]{1,0:T(8,128)S(1)} %pad_maximum_fusion, s32[1024]{0:T(1024)} %pad_clamp_fusion.3), kind=kCustom, calls=%fused_computation.3 | custom fusion | bytes 1475584 | tf_op jit(solution)/shard_map/gather | solution.py:89
  58.5 2.1 %gather_fusion.4 = f32[256,720]{1,0:T(8,128)} fusion(f32[512,720]{1,0:T(8,128)S(1)} %pad_maximum_fusion, s32[1024]{0:T(1024)} %pad_clamp_fusion.2), kind=kCustom, calls=%fused_computation.4 | custom fusion | bytes 1475584 | tf_op jit(solution)/shard_map/gather | solution.py:89
  61.6 2.1 %gather_fusion.5 = f32[256,720]{1,0:T(8,128)} fusion(f32[512,720]{1,0:T(8,128)S(1)} %pad_maximum_fusion, s32[1024]{0:T(1024)} %pad_clamp_fusion.1), kind=kCustom, calls=%fused_computation.5 | custom fusion | bytes 1475584 | tf_op jit(solution)/shard_map/gather | solution.py:89
  65.4 2.2 %gather_fusion.6 = f32[256,720]{1,0:T(8,128)} fusion(f32[512,720]{1,0:T(8,128)S(1)} %pad_maximum_fusion, s32[1024]{0:T(1024)} %pad_clamp_fusion), kind=kCustom, calls=%fused_computation.6 | custom fusion | bytes 1475584 | tf_op jit(solution)/shard_map/gather | solution.py:89
  68.6 1.7 select_multiply_fusion
  71.8 1.1 copy.416
  74.1 1.1 copy.422
  76.3 2.8 %copy.491 = f32[8,384,80]{2,1,0:T(8,128)} copy(f32[8,384,80]{1,2,0:T(8,128)} %all-to-all-done.1) | data formatting | bytes 1966080 | tf_op jit(solution)/shard_map/all_to_all | solution.py:64
  79.2 8.6 %scatter_custom_fusion.2 = f32[1536,80]{1,0:T(8,128)S(1)} fusion(s32[3072]{0:T(1024)} %bitcast.197, f32[3072,80]{1,0:T(8,128)} %bitcast.191, f32[]{:T(128)} %constant.18.clone.1), kind=kCustom, calls=%fused_computation.62 | custom fusion | bytes 492032 | tf_op jit(solution)/shard_map/scatter | solution.py:70
  88.8 2.9 %all_gather.6 = f32[1536,2,80]{0,2,1:T(8,128)S(1)} all-gather(f32[1536,2,40]{0,2,1:T(8,128)} %bitcast.190), channel_id=1, replica_groups=mesh['groups'=2,'cells'=4,'role'=2,'sub'=2] {'sub'}, dimensions={2}, use_global_device_ids=true | all-gather | bytes 1474560 | tf_op jit(solution)/shard_map/all_gather | solution.py:72
  94.7 1.2 copy.429
  100.5 1.1 copy.448
  101.7 1.1 copy.450
  102.8 1.1 copy.455
  104.0 1.1 copy.457
  105.2 1.1 copy.460
  107.5 1.1 copy.464
  108.6 1.1 copy.405
  115.2 7.4 %add_divide_fusion.1 = f32[256,640]{1,0:T(8,128)S(1)} fusion(f32[256,640]{1,0:T(8,128)S(1)} %copy.484, f32[256,640]{1,0:T(8,128)} %copy.425, f32[256,640]{1,0:T(8,128)} %copy.422, f32[256,640]{1,0:T(8,128)} %copy.419, f32[256,640]{1,0:T(8,128)} %copy.416, f32[256,640]{1,0:T(8,128)} %copy.413, f32[256,640]{1,0:T(8,128)S(1)} %copy.408, f32[256,640]{1,0:T(8,128)} %copy.432, ...), kind=kLoop, calls=%fused_computation.43 | loop fusion | flops 14254080 | bytes 20971520 | tf_op jit(solution)/shard_map/div | solution.py:102
  122.6 1.1 gather_fusion.7
  124.5 1.8 collective-permute-start.2
  126.3 2.9 %collective-permute-start.3 = (f32[1,128,640]{2,1,0:T(8,128)S(1)}, f32[1,128,640]{2,1,0:T(8,128)}, u32[]{:S(2)}, u32[]{:S(2)}) collective-permute-start(f32[1,128,640]{2,1,0:T(8,128)S(1)} %get-tuple-element.32), channel_id=1, source_target_pairs={{2,0},{4,2},{6,4},{8,6},{10,8},{12,10},{14,12},{0,14},{3,1},{5,3},... | collective-permute-start | bytes 983048 | tf_op jit(solution)/shard_map/ppermute | solution.py:19
  140.9 2.0 %collective-permute-done.3 = f32[1,128,640]{2,1,0:T(8,128)} collective-permute-done((f32[1,128,640]{2,1,0:T(8,128)S(1)}, f32[1,128,640]{2,1,0:T(8,128)}, u32[]{:S(2)}, u32[]{:S(2)}) %collective-permute-start.3) | collective-permute-done | bytes 327712 | tf_op jit(solution)/shard_map/ppermute | solution.py:19
  142.9 1.2 pad_maximum_fusion.1
  144.0 2.1 %gather_fusion.10 = f32[256,640]{1,0:T(8,128)} fusion(f32[512,640]{1,0:T(8,128)S(1)} %pad_maximum_fusion.1, s32[1024]{0:T(1024)} %pad_clamp_fusion.3), kind=kCustom, calls=%fused_computation.10 | custom fusion | bytes 1311744 | tf_op jit(solution)/shard_map/gather | solution.py:108
  146.1 2.1 %gather_fusion.11 = f32[256,640]{1,0:T(8,128)} fusion(f32[512,640]{1,0:T(8,128)S(1)} %pad_maximum_fusion.1, s32[1024]{0:T(1024)} %pad_clamp_fusion.2), kind=kCustom, calls=%fused_computation.11 | custom fusion | bytes 1311744 | tf_op jit(solution)/shard_map/gather | solution.py:108
  148.2 2.1 %gather_fusion.12 = f32[256,640]{1,0:T(8,128)} fusion(f32[512,640]{1,0:T(8,128)S(1)} %pad_maximum_fusion.1, s32[1024]{0:T(1024)} %pad_clamp_fusion.1), kind=kCustom, calls=%fused_computation.12 | custom fusion | bytes 1311744 | tf_op jit(solution)/shard_map/gather | solution.py:108
  150.3 2.0 %gather_fusion.8 = f32[256,640]{1,0:T(8,128)} fusion(f32[512,640]{1,0:T(8,128)S(1)} %pad_maximum_fusion.1, s32[1024]{0:T(1024)S(1)} %pad_clamp_fusion.5), kind=kCustom, calls=%fused_computation.8 | custom fusion | bytes 1311744 | tf_op jit(solution)/shard_map/gather | solution.py:108
  152.3 2.0 %gather_fusion.9 = f32[256,640]{1,0:T(8,128)} fusion(f32[512,640]{1,0:T(8,128)S(1)} %pad_maximum_fusion.1, s32[1024]{0:T(1024)} %pad_clamp_fusion.4), kind=kCustom, calls=%fused_computation.9 | custom fusion | bytes 1311744 | tf_op jit(solution)/shard_map/gather | solution.py:108
  154.3 2.2 %gather_fusion.13 = f32[256,640]{1,0:T(8,128)} fusion(f32[512,640]{1,0:T(8,128)S(1)} %pad_maximum_fusion.1, s32[1024]{0:T(1024)} %pad_clamp_fusion), kind=kCustom, calls=%fused_computation.13 | custom fusion | bytes 1311744 | tf_op jit(solution)/shard_map/gather | solution.py:108
  156.5 10.5 %add_subtract_fusion = f32[256,640]{1,0:T(8,128)S(1)} fusion(f32[256,640]{1,0:T(8,128)S(1)} %copy.484, f32[256,640]{1,0:T(8,128)} %copy.425, f32[256,640]{1,0:T(8,128)} %copy.482, f32[256,640]{1,0:T(8,128)} %gather_fusion.13, f32[256,640]{1,0:T(8,128)} %copy.422, f32[256,640]{1,0:T(8,128)} %copy.479, f32[256,640]{1,0:T(8,128)} %gather_fusion.12, ...), kind=kLoop, calls=%fused_computation.42 | loop fusion | flops 22118400 | bytes 28835840 | tf_op jit(solution)/shard_map/sub | solution.py:110
  169.5 10.1 %all-gather.2.cloned.1.call-done = f32[256,1280]{1,0:T(8,128)} async-done(((f32[256,640]{1,0:T(8,128)}), f32[256,1280]{1,0:T(8,128)}) %all-gather.2.cloned.1.call-update) | async-done | bytes 1310736 | tf_op jit(solution)/shard_map/all_gather | solution.py:123
  179.6 1.5 add_divide_fusion
  182.0 1.5 fusion.5
  (187 shorter events, 51.0 us)
Async XLA Ops:
  6.5 175.0 %copy-start = (f32[16,16]{1,0:T(8,128)S(1)}, f32[16,16]{1,0:T(8,128)}, u32[]{:S(2)}) copy-start(f32[16,16]{1,0:T(8,128)} %param.21) | copy-start | bytes 3076
  6.5 2.1 %copy-start.35 = (s32[2,128]{1,0:T(2,128)S(1)}, s32[2,128]{1,0:T(2,128)}, u32[]{:S(2)}) copy-start(s32[2,128]{1,0:T(2,128)} %param.14) | copy-start | bytes 3076
  9.9 7.0 %copy-start.26 = (s32[1536]{0:T(1024)S(1)}, s32[1536]{0:T(1024)}, u32[]{:S(2)}) copy-start(s32[1536]{0:T(1024)} %param.17) | copy-start | bytes 18436
  9.9 20.7 %copy-start.28 = (s32[6,256]{1,0:T(8,128)S(1)}, s32[6,256]{1,0:T(8,128)}, u32[]{:S(2)}) copy-start(s32[6,256]{1,0:T(8,128)} %param.13) | copy-start | bytes 18436
  9.9 21.3 %copy-start.24 = (f32[40,1536]{1,0:T(8,128)S(1)}, f32[40,1536]{1,0:T(8,128)}, u32[]{:S(2)}) copy-start(f32[40,1536]{1,0:T(8,128)} %param.16) | copy-start | bytes 737284
  9.9 21.2 %copy-start.25 = (f32[40,1536]{1,0:T(8,128)S(1)}, f32[40,1536]{1,0:T(8,128)}, u32[]{:S(2)}) copy-start(f32[40,1536]{1,0:T(8,128)} %param.15) | copy-start | bytes 737284
  10.8 39.1 %collective-permute-start = (f32[1,128,720]{2,1,0:T(8,128)}, f32[1,128,720]{2,1,0:T(8,128)S(1)}, u32[]{:S(2)}, u32[]{:S(2)}) collective-permute-start(f32[1,128,720]{2,1,0:T(8,128)} %get-tuple-element.29), channel_id=1, source_target_pairs={{0,2},{2,4},{4,6},{6,8},{8,10},{10,12},{12,14},{14,0},{1,3},{3,5},... | collective-permute-start | bytes 1105928 | tf_op jit(solution)/shard_map/ppermute | solution.py:16
  13.8 36.2 %collective-permute-start.1 = (f32[1,128,720]{2,1,0:T(8,128)}, f32[1,128,720]{2,1,0:T(8,128)}, u32[]{:S(2)}, u32[]{:S(2)}) collective-permute-start(f32[1,128,720]{2,1,0:T(8,128)} %get-tuple-element.30), channel_id=1, source_target_pairs={{2,0},{4,2},{6,4},{8,6},{10,8},{12,10},{14,12},{0,14},{3,1},{5,3},... | collective-permute-start | bytes 1105928 | tf_op jit(solution)/shard_map/ppermute | solution.py:19
  19.7 12.0 %copy-start.27 = (s32[1536]{0:T(1024)}, s32[1536]{0:T(1024)S(1)}, u32[]{:S(2)}) copy-start(s32[1536]{0:T(1024)S(1)} %compare_select_fusion.1) | copy-start | bytes 18436
  26.7 12.2 %all-to-all-start = ((s32[8,384,1]{1,2,0:T(1,128)}), s32[8,384,1]{1,2,0:T(1,128)}, u32[]{:S(2)}, u32[]{:S(2)}) async-start(s32[8,384,1]{1,2,0:T(1,128)} %bitcast.13), calls=%async_computation | async-start | bytes 24576 | tf_op jit(solution)/shard_map/all_to_all | solution.py:65
  38.9 6.7 %copy-start.34 = (s32[256,1]{0,1:T(1,128)S(1)}, s32[256,1]{0,1:T(1,128)}, u32[]{:S(2)}) copy-start(s32[256,1]{0,1:T(1,128)} %get-tuple-element.36) | copy-start | bytes 3076
  38.9 7.3 %copy-start.33 = (s32[256,1]{0,1:T(1,128)S(1)}, s32[256,1]{0,1:T(1,128)}, u32[]{:S(2)}) copy-start(s32[256,1]{0,1:T(1,128)} %get-tuple-element.35) | copy-start | bytes 3076
  38.9 7.9 %copy-start.32 = (s32[256,1]{0,1:T(1,128)S(1)}, s32[256,1]{0,1:T(1,128)}, u32[]{:S(2)}) copy-start(s32[256,1]{0,1:T(1,128)} %get-tuple-element.34) | copy-start | bytes 3076
  38.9 8.5 %copy-start.31 = (s32[256,1]{0,1:T(1,128)S(1)}, s32[256,1]{0,1:T(1,128)}, u32[]{:S(2)}) copy-start(s32[256,1]{0,1:T(1,128)} %get-tuple-element.38) | copy-start | bytes 3076
  38.9 9.1 %copy-start.30 = (s32[256,1]{0,1:T(1,128)S(1)}, s32[256,1]{0,1:T(1,128)}, u32[]{:S(2)}) copy-start(s32[256,1]{0,1:T(1,128)} %get-tuple-element.37) | copy-start | bytes 3076
  38.9 37.4 %all-to-all-start.1 = ((f32[8,384,80]{1,2,0:T(8,128)}), f32[8,384,80]{1,2,0:T(8,128)}, u32[]{:S(2)}, u32[]{:S(2)}) async-start(f32[8,384,80]{1,2,0:T(8,128)} %copy.401), calls=%async_computation.1 | async-start | bytes 1966080 | tf_op jit(solution)/shard_map/all_to_all | solution.py:64
  44.8 134.8 %all-gather.2.cloned.1.call-start = ((), (), s32[]{:S(2)}) async-start(), calls=%async_computation.2 | async-start | bytes 1966080 | tf_op jit(solution)/shard_map/all_gather | solution.py:123
  65.3 3.3 %copy-start.7 = (f32[256,79]{0,1:T(8,128)S(1)}, f32[256,79]{0,1:T(8,128)}, u32[]{:S(2)}) copy-start(f32[256,79]{0,1:T(8,128)} %slice.249) | copy-start | bytes 242692
  65.3 3.3 %copy-start.29 = (s32[256]{0:T(256)S(1)}, s32[256]{0:T(256)}, u32[]{:S(2)}) copy-start(s32[256]{0:T(256)} %param.12) | copy-start | bytes 3076
  65.3 3.3 %copy-start.36 = (pred[80]{0:T(512)(128)(4,1)S(1)}, pred[80]{0:T(512)(128)(4,1)}, u32[]{:S(2)}) copy-start(pred[80]{0:T(512)(128)(4,1)} %iota_compare_fusion.3) | copy-start | bytes 244
  65.3 3.3 %copy-start.37 = (f32[80]{0:T(128)S(1)}, f32[80]{0:T(128)}, u32[]{:S(2)}) copy-start(f32[80]{0:T(128)} %multiply_exponential_fusion) | copy-start | bytes 964
  70.6 44.6 %copy-start.3 = (f32[256,640]{1,0:T(8,128)}, f32[256,640]{1,0:T(8,128)S(1)}, u32[]{:S(2)}) copy-start(f32[256,640]{1,0:T(8,128)S(1)} %copy.408) | copy-start | bytes 1966084
  93.5 1.1 copy-start.19
  93.6 2.3 %copy-start.18 = (f32[256,80]{0,1:T(8,128)S(1)}, f32[256,80]{0,1:T(8,128)}, u32[]{:S(2)}) copy-start(f32[256,80]{0,1:T(8,128)} %get-tuple-element.8) | copy-start | bytes 245764
  94.7 2.3 %copy-start.17 = (f32[256,80]{0,1:T(8,128)S(1)}, f32[256,80]{0,1:T(8,128)}, u32[]{:S(2)}) copy-start(f32[256,80]{0,1:T(8,128)} %get-tuple-element.9) | copy-start | bytes 245764
  95.9 2.2 %copy-start.16 = (f32[256,80]{0,1:T(8,128)S(1)}, f32[256,80]{0,1:T(8,128)}, u32[]{:S(2)}) copy-start(f32[256,80]{0,1:T(8,128)} %get-tuple-element.10) | copy-start | bytes 245764
  97.1 2.2 %copy-start.15 = (f32[256,80]{0,1:T(8,128)S(1)}, f32[256,80]{0,1:T(8,128)}, u32[]{:S(2)}) copy-start(f32[256,80]{0,1:T(8,128)} %get-tuple-element.11) | copy-start | bytes 245764
  98.2 2.2 %copy-start.14 = (f32[256,80]{0,1:T(8,128)S(1)}, f32[256,80]{0,1:T(8,128)}, u32[]{:S(2)}) copy-start(f32[256,80]{0,1:T(8,128)} %get-tuple-element.12) | copy-start | bytes 245764
  99.4 2.3 %copy-start.13 = (f32[256,80]{0,1:T(8,128)S(1)}, f32[256,80]{0,1:T(8,128)}, u32[]{:S(2)}) copy-start(f32[256,80]{0,1:T(8,128)} %get-tuple-element.13) | copy-start | bytes 245764
  106.3 2.3 %copy-start.23 = (f32[256,80]{0,1:T(8,128)S(1)}, f32[256,80]{0,1:T(8,128)}, u32[]{:S(2)}) copy-start(f32[256,80]{0,1:T(8,128)} %get-tuple-element.28) | copy-start | bytes 245764
  107.5 2.3 %copy-start.22 = (f32[256,80]{0,1:T(8,128)S(1)}, f32[256,80]{0,1:T(8,128)}, u32[]{:S(2)}) copy-start(f32[256,80]{0,1:T(8,128)} %get-tuple-element.27) | copy-start | bytes 245764
  108.6 2.3 %copy-start.21 = (f32[256,80]{0,1:T(8,128)S(1)}, f32[256,80]{0,1:T(8,128)}, u32[]{:S(2)}) copy-start(f32[256,80]{0,1:T(8,128)} %get-tuple-element.24) | copy-start | bytes 245764
  109.8 2.2 %copy-start.20 = (f32[256,80]{0,1:T(8,128)S(1)}, f32[256,80]{0,1:T(8,128)}, u32[]{:S(2)}) copy-start(f32[256,80]{0,1:T(8,128)} %get-tuple-element.26) | copy-start | bytes 245764
  112.1 3.1 %copy-start.1 = (f32[256,720]{1,0:T(8,128)S(1)}, f32[256,720]{1,0:T(8,128)}, u32[]{:S(2)}) copy-start(f32[256,720]{1,0:T(8,128)} %gather_fusion.2) | copy-start | bytes 2211844
  122.6 6.6 %copy-start.9 = (f32[256,80]{0,1:T(8,128)S(1)}, f32[256,80]{0,1:T(8,128)}, u32[]{:S(2)}) copy-start(f32[256,80]{0,1:T(8,128)} %get-tuple-element.40) | copy-start | bytes 245764
  124.5 16.4 %collective-permute-start.2 = (f32[1,128,640]{2,1,0:T(8,128)}, f32[1,128,640]{2,1,0:T(8,128)S(1)}, u32[]{:S(2)}, u32[]{:S(2)}) collective-permute-start(f32[1,128,640]{2,1,0:T(8,128)} %get-tuple-element.31), channel_id=1, source_target_pairs={{0,2},{2,4},{4,6},{6,8},{8,10},{10,12},{12,14},{14,0},{1,3},{3,5},... | collective-permute-start | bytes 983048 | tf_op jit(solution)/shard_map/ppermute | solution.py:16
  126.3 16.6 %collective-permute-start.3 = (f32[1,128,640]{2,1,0:T(8,128)S(1)}, f32[1,128,640]{2,1,0:T(8,128)}, u32[]{:S(2)}, u32[]{:S(2)}) collective-permute-start(f32[1,128,640]{2,1,0:T(8,128)S(1)} %get-tuple-element.32), channel_id=1, source_target_pairs={{2,0},{4,2},{6,4},{8,6},{10,8},{12,10},{14,12},{0,14},{3,1},{5,3},... | collective-permute-start | bytes 983048 | tf_op jit(solution)/shard_map/ppermute | solution.py:19
  129.3 3.1 %copy-start.12 = (f32[256,80]{0,1:T(8,128)S(1)}, f32[256,80]{0,1:T(8,128)}, u32[]{:S(2)}) copy-start(f32[256,80]{0,1:T(8,128)} %get-tuple-element.22) | copy-start | bytes 245764
  132.4 3.1 %copy-start.11 = (f32[256,80]{0,1:T(8,128)S(1)}, f32[256,80]{0,1:T(8,128)}, u32[]{:S(2)}) copy-start(f32[256,80]{0,1:T(8,128)} %get-tuple-element.20) | copy-start | bytes 245764
  135.6 3.1 %copy-start.10 = (f32[256,80]{0,1:T(8,128)S(1)}, f32[256,80]{0,1:T(8,128)}, u32[]{:S(2)}) copy-start(f32[256,80]{0,1:T(8,128)} %get-tuple-element.18) | copy-start | bytes 245764
  140.9 2.0 %copy-start.8 = (f32[1,128,640]{2,1,0:T(8,128)}, f32[1,128,640]{2,1,0:T(8,128)S(1)}, u32[]{:S(2)}) copy-start(f32[1,128,640]{2,1,0:T(8,128)S(1)} %collective-permute-done.2) | copy-start | bytes 983044
  154.3 2.2 %copy-start.4 = (f32[256,640]{1,0:T(8,128)S(1)}, f32[256,640]{1,0:T(8,128)}, u32[]{:S(2)}) copy-start(f32[256,640]{1,0:T(8,128)} %copy-done.3) | copy-start | bytes 1966084
  167.0 1.1 copy-start.5
  168.2 1.1 copy-start.38
  181.1 0.9 copy-start.6
  183.6 1.1 copy-start.2
Sparse Core Ops, SparseCore 0:
  169.5 10.1 all-gather.1
where the time goes:
time: 194 us; the launch traced here: 193 us
  local copies, waits for them, and re-layouts  104 us (54%)
  other arithmetic  35.6 us (18%)
  starting transfers between devices  20.7 us (11%)
  between operations  14.3 us (7%)
  waiting for transfers between devices  13.2 us (7%)
  blocking collectives  2.93 us (2%)
    gather x6, local copies, waits for them, and re-layouts, body(): bound = jnp.minimum(limiter_ratio, limit_ext[neighbor[slot_index]])  12.5 us
    gather x6, local copies, waits for them, and re-layouts, body(): gathered = extended[nb_cells]  11.8 us
    sub x1, other arithmetic, body(): advected = field - net_flux  10.5 us
    all_gather x1, waiting for transfers between devices, body(): every = lax.all_gather(mixed_field, 'sub', axis=1, tiled=True)  10.1 us
    scatter x2, local copies, waits for them, and re-layouts, body(): edge_table = jnp.zeros((record_count, payload_cols), jnp.float32).at[arri...  9.67 us
    another operation x12, local copies, waits for them, and re-layouts, body(): kappa_flat = jnp.tile(kappa_edges[slot_index], (1, tracer_count))  9.41 us
    div x1, other arithmetic, body(): limiter_ratio = spread / (spread + total_abs + LIMIT_PAD)  7.36 us
    scatter x1, local copies, waits for them, and re-layouts, body(): jnp.full((blocks * capacity,), record_count, jnp.int32).at[target]  6.92 us
  transfers between devices with their start and end apart: 7, of which 3 were waited for; matrix products, arithmetic and copies ran while one was open for 31% of the time, Pallas kernels for 0%

commit v1 on v0

v1 whole, which is shorter than its diff:
```python
import functools

import jax
import jax.numpy as jnp
from jax import lax
from jax.experimental import pallas as pl
from jax.experimental.pallas import tpu as pltpu
from jax.sharding import PartitionSpec as P

LIMIT_PAD = 1.5
REACT_RATE = 0.5
F32 = jnp.float32
BF16 = jnp.bfloat16
MESH = pl.DeviceIdType.MESH
NT_DIMS = (((1,), (1,)), ((), ()))


def steps(count, fn):
    if count <= 8:
        for i in range(count):
            fn(i)
    else:
        lax.fori_loop(0, count, lambda i, c: (fn(i), c)[1], 0)


def dot(a, b):
    return jnp.dot(a, b, preferred_element_type=F32)


def dot_nt(a, b):
    return lax.dot_general(a, b, NT_DIMS, preferred_element_type=F32)


def split(x):
    hi = x.astype(BF16)
    return hi, (x - hi.astype(F32)).astype(BF16)


def onehot(cond):
    return jnp.where(cond, 1.0, 0.0).astype(BF16)


def kernel(
    blocks, n_role, cap,
    tr_ref, lc_ref, nb_ref, halo_ref, tp_ref, ed_ref, dest_ref, slot_ref, vd_ref,
    hs_ref, st_ref,
    out_ref,
    field, rec_a, send, arrived, flow, xa, la, gsel, hsel, pk, lk, lim, adv, edge_out, edge_in,
    rim_out, rim_in, lrim_out, lrim_in, res, masks, terms,
    send_sem, recv_sem, tr_sem, rim_send, rim_recv, lrim_send, lrim_recv, edge_sem, res_sem,
):
    own, layers, cells = tr_ref.shape
    half = layers // 2
    tracers = 2 * own
    rows = tracers * half
    cols = halo_ref.shape[1]
    ext = cells + 2 * cols
    recs = dest_ref.shape[1]
    slots = 6 * cells
    sub = lax.axis_index("sub")
    me = lax.axis_index("cells") * n_role + lax.axis_index("role")
    other = {"sub": 1 - sub}

    def at(block):
        return {"cells": block // n_role, "role": lax.rem(block, n_role)}

    def partner(d):
        return lax.rem(me + d, blocks)

    barrier = pltpu.get_barrier_semaphore()

    def greet(i):
        pl.semaphore_signal(barrier, inc=1, device_id=at(partner(i + 1)), device_id_type=MESH)

    steps(blocks - 1, greet)
    pl.semaphore_signal(barrier, inc=1, device_id=other, device_id_type=MESH)
    pl.semaphore_wait(barrier, blocks)

    mine = pl.multiple_of(sub * half, half)
    theirs = pl.multiple_of((1 - sub) * half, half)

    tr_copy = pltpu.make_async_remote_copy(
        src_ref=tr_ref.at[:, pl.ds(theirs, half), :],
        dst_ref=field.at[pl.ds(sub * own, own)],
        send_sem=tr_sem.at[0], recv_sem=tr_sem.at[1],
        device_id=other, device_id_type=MESH,
    )
    tr_copy.start()

    dest = dest_ref[...]
    block_id = lax.broadcasted_iota(jnp.int32, (max(blocks, 8), recs), 0)
    match = jnp.where(block_id == dest, 1.0, 0.0)
    chunk = 256
    before = onehot(
        lax.broadcasted_iota(jnp.int32, (chunk, chunk), 0)
        < lax.broadcasted_iota(jnp.int32, (chunk, chunk), 1)
    )
    carry = jnp.zeros((match.shape[0], 1), F32)
    ranks = []
    for c in range(recs // chunk):
        part = match[:, c * chunk:(c + 1) * chunk]
        rank = dot(part.astype(BF16), before) + carry
        ranks.append(jnp.sum(rank * part, axis=0, keepdims=True))
        carry = carry + jnp.sum(part, axis=1, keepdims=True)
    rank = jnp.concatenate(ranks, axis=1).astype(jnp.int32)
    target = dest * cap + rank

    slot_rows = jnp.broadcast_to(slot_ref[...].astype(F32) + 1.0, (8, recs))
    payload = jnp.concatenate([tp_ref[...], ed_ref[...], slot_rows], axis=0)
    width = payload.shape[0]
    top = payload.astype(BF16).astype(F32)
    rec_a[...] = jnp.concatenate([top, payload - top], axis=0).astype(BF16)

    place = lax.broadcasted_iota(jnp.int32, (cap, recs), 0)

    def pack(block):
        sel = onehot(place == target - block * cap)
        both = dot_nt(rec_a[...], sel)
        return both[:width] + both[width:]

    def rec_copy(block, source):
        return pltpu.make_async_remote_copy(
            src_ref=send.at[block], dst_ref=arrived.at[source],
            send_sem=send_sem.at[block], recv_sem=recv_sem.at[source],
            device_id=at(block), device_id_type=MESH,
        )

    order = (4, 3, 5, 2, 6, 1, 7)

    def offset(i):
        return order[i] if blocks == 8 else i + 1

    def ship(i):
        block = partner(offset(i))
        send[block] = pack(block)
        rec_copy(block, me).start()

    steps(blocks - 1, ship)
    arrived[me] = pack(me)

    local_rows = lax.broadcasted_iota(jnp.int32, (cells, cols), 0)
    for side in range(2):
        sel = onehot(local_rows == halo_ref[side:side + 1, :])
        hsel[0:cells, side * cols:(side + 1) * cols] = sel
        hsel[cells:2 * cells, side * cols:(side + 1) * cols] = sel
    ext_rows = lax.broadcasted_iota(jnp.int32, (ext, cells), 0)
    for k in range(6):
        sel = onehot(ext_rows == nb_ref[k:k + 1, :])
        gsel[k, 0:ext, :] = sel
        gsel[k, ext:2 * ext, :] = sel

    field[pl.ds(sub * own, own)] = tr_ref[:, pl.ds(mine, half), :]
    tr_copy.wait()
    whole = field[...].reshape(rows, cells)
    hi, lo = split(whole)
    xa[:, 0:cells] = hi
    xa[:, ext:ext + cells] = lo
    picked = dot(hi, hsel[0:cells]) + dot(lo, hsel[cells:2 * cells])
    count = jnp.broadcast_to(lc_ref[...].astype(F32), (8, cells))
    picked_count = dot(count.astype(BF16), hsel[0:cells])
    for side in range(2):
        rim_out[side, 0:rows] = picked[:, side * cols:(side + 1) * cols]
        rim_out[side, rows:rows + 8] = picked_count[:, side * cols:(side + 1) * cols]

    def rim_copies(out, into, s_sem, r_sem):
        result = []
        for side in range(2):
            to = partner(blocks - 1 if side == 0 else 1)
            result.append(pltpu.make_async_remote_copy(
                src_ref=out.at[side], dst_ref=into.at[1 - side],
                send_sem=s_sem.at[side], recv_sem=r_sem.at[1 - side],
                device_id=at(to), device_id_type=MESH,
            ))
        return result

    rims = rim_copies(rim_out, rim_in, rim_send, rim_recv)
    for copy in rims:
        copy.start()
    for copy in rims:
        copy.wait_recv()

    layer = lax.broadcasted_iota(jnp.int32, (half, cells), 0) + sub * half
    wet = jnp.where(layer < lc_ref[...], 1.0, 0.0)
    layer_f = layer.astype(F32)
    count_ext = jnp.concatenate(
        [count, rim_in[0, rows:rows + 8], rim_in[1, rows:rows + 8]], axis=1
    ).astype(BF16)
    for side in range(2):
        hi, lo = split(rim_in[side, 0:rows])
        first = cells + side * cols
        xa[:, first:first + cols] = hi
        xa[:, ext + first:ext + first + cols] = lo
    for k in range(6):
        pk[k] = dot(xa[...], gsel[k])
        far_count = dot(count_ext, gsel[k, 0:ext])[0:1]
        masks[k] = jnp.where(layer_f < far_count, wet, 0.0)

    flow[...] = jnp.zeros_like(flow)
    slot_id = lax.broadcasted_iota(jnp.int32, (slots, cap), 0).astype(F32) + 1.0

    def unpack(block):
        got = arrived[block]
        sel = onehot(slot_id == got[width - 8:width - 7, :])
        body = got[:width - 8]
        top = body.astype(BF16).astype(F32)
        both = dot_nt(jnp.concatenate([top, body - top], axis=0).astype(BF16), sel)
        flow[...] += both[:width - 8] + both[width - 8:]

    unpack(me)

    def take(i):
        block = partner(blocks - offset(i))
        rec_copy(block, block).wait_recv()
        unpack(block)

    steps(blocks - 1, take)

    total = jnp.zeros((half, cells), F32)
    for k in range(6):
        u = flow[0:half, k * cells:(k + 1) * cells] * masks[k]
        kap = flow[half:2 * half, k * cells:(k + 1) * cells] * masks[k]
        terms[k] = 0.5 * jnp.abs(u)
        terms[6 + k] = jnp.minimum(u, 0.0) - kap
        total = total + u
    terms[12] = total

    def limiter(t, c):
        q = field[t]
        here = pl.ds(pl.multiple_of(t * half, half), half)
        high = jnp.zeros_like(q)
        low = jnp.zeros_like(q)
        size = jnp.zeros_like(q)
        for k in range(6):
            d = (pk[k, here, :] - q) * masks[k]
            pk[k, here, :] = d
            high = jnp.maximum(high, d)
            low = jnp.minimum(low, d)
            size = size + terms[k] * jnp.abs(d)
        spread = high - low
        lim[here, :] = spread / (spread + size + LIMIT_PAD)
        return c

    lax.fori_loop(0, tracers, limiter, 0)

    hi, lo = split(lim[...])
    la[:, 0:cells] = hi
    la[:, ext:ext + cells] = lo
    picked = dot(hi, hsel[0:cells]) + dot(lo, hsel[cells:2 * cells])
    for side in range(2):
        lrim_out[side] = picked[:, side * cols:(side + 1) * cols]
    lrims = rim_copies(lrim_out, lrim_in, lrim_send, lrim_recv)
    for copy in lrims:
        copy.start()
    for copy in lrims:
        copy.wait_recv()
    for side in range(2):
        hi, lo = split(lrim_in[side])
        first = cells + side * cols
        la[:, first:first + cols] = hi
        la[:, ext + first:ext + first + cols] = lo
    for k in range(6):
        lk[k] = dot(la[...], gsel[k])

    def advect(t, c):
        q = field[t]
        here = pl.ds(pl.multiple_of(t * half, half), half)
        own_lim = lim[here, :]
        net = q * terms[12]
        for k in range(6):
            bound = jnp.minimum(own_lim, lk[k, here, :])
            net = net + pk[k, here, :] * (terms[6 + k] + bound * terms[k])
        adv[t] = q - net
        return c

    lax.fori_loop(0, tracers, advect, 0)

    @pl.when(sub == 0)
    def _():
        edge_out[...] = adv[:, half - 1, :]

    @pl.when(sub == 1)
    def _():
        edge_out[...] = adv[:, 0, :]

    edge_copy = pltpu.make_async_remote_copy(
        src_ref=edge_out, dst_ref=edge_in, send_sem=edge_sem.at[0], recv_sem=edge_sem.at[1],
        device_id=other, device_id_type=MESH,
    )
    edge_copy.start()
    edge_copy.wait()

    counts = lc_ref[...]
    upper = vd_ref[pl.ds(mine, half), :]
    w_down = jnp.where(
        (layer < layers - 1) & (layer + 1 < counts), upper, 0.0
    )
    cut = jnp.where(half < counts, vd_ref[half - 1:half, :], 0.0)
    row = lax.broadcasted_iota(jnp.int32, (half, cells), 0)
    w_up = jnp.where(row == 0, jnp.where(sub == 0, 0.0, cut), pltpu.roll(w_down, 1, 0))
    light = REACT_RATE * jnp.exp(-3.0 * layer_f / layers) * wet

    def mix(t, c):
        a = adv[t]
        across = edge_in[pl.ds(t, 1), :]
        below = jnp.where(row == half - 1, across, pltpu.roll(a, half - 1, 0))
        above = jnp.where(row == 0, across, pltpu.roll(a, 1, 0))
        m = a + w_down * (below - a) - w_up * (a - above)
        adv[t] = m
        sq = m * m
        field[t] = sq / (hs_ref[t] + sq)
        return c

    lax.fori_loop(0, tracers, mix, 0)

    def react(t):
        acc = st_ref[t, 0] * field[0]
        for s in range(1, tracers):
            acc = acc + st_ref[t, s] * field[s]
        return adv[t] + light * acc

    def far(i, c):
        res[i] = react((1 - sub) * own + i)
        return c

    def near(i, c):
        out_ref[i, pl.ds(mine, half), :] = react(sub * own + i)
        return c

    lax.fori_loop(0, own, far, 0)
    res_copy = pltpu.make_async_remote_copy(
        src_ref=res, dst_ref=out_ref.at[:, pl.ds(mine, half), :],
        send_sem=res_sem.at[0], recv_sem=res_sem.at[1],
        device_id=other, device_id_type=MESH,
    )
    res_copy.start()
    lax.fori_loop(0, own, near, 0)
    res_copy.wait()

    def drain(i):
        rec_copy(partner(i + 1), me).wait_send()

    steps(blocks - 1, drain)
    for copy in rims + lrims:
        copy.wait_send()


def body(
    tracers, layer_count, neighbor, halo_cells, transport, edge_diff,
    record_dest, record_slot, vert_diff, half_sat, stoich,
):
    own, layers, cells = tracers.shape
    half = layers // 2
    count = 2 * own
    rows = count * half
    cols = halo_cells.shape[1]
    recs = record_dest.shape[0]
    ext = cells + 2 * cols
    n_role = lax.axis_size("role")
    blocks = lax.axis_size("cells") * n_role
    cap = -(-(2 * recs // blocks) // 128) * 128
    width = layers + 8
    vmem = pl.BlockSpec(memory_space=pltpu.VMEM)
    smem = pl.BlockSpec(memory_space=pltpu.SMEM)
    pair = pltpu.SemaphoreType.DMA((2,))
    return pl.pallas_call(
        functools.partial(kernel, blocks, n_role, cap),
        out_shape=jax.ShapeDtypeStruct(tracers.shape, F32),
        in_specs=[vmem] * 9 + [smem] * 2,
        out_specs=vmem,
        scratch_shapes=[
            pltpu.VMEM((count, half, cells), F32),
            pltpu.VMEM((2 * width, recs), BF16),
            pltpu.VMEM((blocks, width, cap), F32),
            pltpu.VMEM((blocks, width, cap), F32),
            pltpu.VMEM((layers, 6 * cells), F32),
            pltpu.VMEM((rows, 2 * ext), BF16),
            pltpu.VMEM((rows, 2 * ext), BF16),
            pltpu.VMEM((6, 2 * ext, cells), BF16),
            pltpu.VMEM((2 * cells, 2 * cols), BF16),
            pltpu.VMEM((6, rows, cells), F32),
            pltpu.VMEM((6, rows, cells), F32),
            pltpu.VMEM((rows, cells), F32),
            pltpu.VMEM((count, half, cells), F32),
            pltpu.VMEM((count, cells), F32),
            pltpu.VMEM((count, cells), F32),
            pltpu.VMEM((2, rows + 8, cols), F32),
            pltpu.VMEM((2, rows + 8, cols), F32),
            pltpu.VMEM((2, rows, cols), F32),
            pltpu.VMEM((2, rows, cols), F32),
            pltpu.VMEM((own, half, cells), F32),
            pltpu.VMEM((6, half, cells), F32),
            pltpu.VMEM((13, half, cells), F32),
            pltpu.SemaphoreType.DMA((blocks,)),
            pltpu.SemaphoreType.DMA((blocks,)),
            pair, pair, pair, pair, pair, pair, pair,
        ],
        compiler_params=pltpu.CompilerParams(
            collective_id=0, has_side_effects=True, vmem_limit_bytes=52 * 1024 * 1024
        ),
        name="tracer_step",
    )(
        tracers, layer_count.reshape(1, -1), neighbor, halo_cells, transport, edge_diff,
        record_dest.reshape(1, -1), record_slot.reshape(1, -1), vert_diff, half_sat, stoich,
    )


def solution(mesh):
    in_specs = (
        P("sub", None, ("groups", "cells", "role")),
        P(("groups", "cells", "role")),
        P(None, ("groups", "cells", "role")),
        P(None, ("groups", "cells", "role")),
        P("sub", ("groups", "cells", "role")),
        P("sub", ("groups", "cells", "role")),
        P(("groups", "cells", "role")),
        P(("groups", "cells", "role")),
        P(None, ("groups", "cells", "role")),
        P(),
        P(),
    )
    out_specs = P("sub", None, ("groups", "cells", "role"))
    return jax.shard_map(body, mesh=mesh, in_specs=in_specs, out_specs=out_specs, check_vma=False)
```

time: 194 us -> 73.6 us (0.38)
  local copies, waits for them, and re-layouts: 104 us -> 6.1 us
  Pallas kernels: 0 us -> 67.1 us
  other arithmetic: 35.6 us -> 0 us
  starting transfers between devices: 20.7 us -> 0 us
  between operations: 14.3 us -> 0.06 us
  waiting for transfers between devices: 13.2 us -> 0 us
  blocking collectives: 2.93 us -> 0 us
    pallas_call x0 -> x1, Pallas kernels: none -> 67.1 us  [body(): pl.pallas_call(functools.partial(kernel, blocks, n_role, cap), out_shape=...]
    gather x14 -> x0, local copies, waits for them, and re-layouts: 26.4 us -> none  [the longest x6 12.5 us: body(): bound = jnp.minimum(limiter_ratio, limit_ext[neighbor[slot_index]])]
    scatter x4 -> x0, local copies, waits for them, and re-layouts: 21.4 us -> none  [the longest x2 9.67 us: body(): edge_table = jnp.zeros((record_count, payload_cols), jnp.float32).at[arri...]
    mul x14 -> x0, local copies, waits for them, and re-layouts: 12.7 us -> none  [the longest x6 6.58 us: edge_terms(): antidiff = open_mask * (0.5 * flow * (field + beyond)) - upwind]
    another operation x38 -> x0, local copies, waits for them, and re-layouts: 12.6 us -> none  [the longest x12 9.41 us: body(): kappa_flat = jnp.tile(kappa_edges[slot_index], (1, tracer_count))]
    sub x2 -> x0, other arithmetic: 11.6 us -> none  [the longest x1 10.5 us: body(): advected = field - net_flux]
    ppermute x4 -> x0, starting transfers between devices: 10.7 us -> none  [the longest x2 5.96 us: extended_2(): lax.ppermute(lax.slice_in_dim(block, 0, width, axis=dim), axis, backward)]
    all_gather x1 -> x0, waiting for transfers between devices: 10.1 us -> none  [body(): every = lax.all_gather(mixed_field, 'sub', axis=1, tiled=True)]
  transfers between devices with their start and end apart: 7 -> 0, of which waited for: 3 -> 0; matrix products, arithmetic and copies ran while one was open for 31% -> 0% of each run, Pallas kernels for 0% -> 0%
where the time goes in v1:
time: 73.6 us; the launch traced here: 73.2 us
  Pallas kernels  67.1 us (91%)
  local copies, waits for them, and re-layouts  6.1 us (8%)
    pallas_call x1, Pallas kernels, body(): pl.pallas_call(functools.partial(kernel, blocks, n_role, cap), out_shape=...  67.1 us
    unnamed x21, local copies, waits for them, and re-layouts  5.37 us

profile of v1, /device:TPU:0, one launch (start us, length us, event | category | flops | bytes accessed | tf_op | source)
XLA Modules:
  0.0 73.2 jit_solution(3863767661701040486)
XLA Ops:
  0.0 0.0 copy-start.9
  0.0 0.0 copy-start.5
  0.0 0.7 reshape.10.dest_ref
  0.7 0.0 copy-done.9
  0.7 0.0 copy-start.4
  0.7 0.0 copy-start.6
  0.8 0.0 copy-start.7
  0.8 0.0 copy-start.8
  0.8 0.0 copy-done.5
  0.8 0.6 copy-done.4
  1.4 0.0 copy-done.6
  1.4 0.0 copy-done.7
  1.4 0.0 copy-done.8
  1.5 0.0 copy-start
  1.5 1.1 %copy-done = f32[8,80,256]{2,1,0:T(8,128)S(1)} copy-done((f32[8,80,256]{2,1,0:T(8,128)S(1)}, f32[8,80,256]{2,1,0:T(8,128)}, u32[]{:S(2)}) %copy-start) | copy-done | bytes 655384
  2.5 0.0 copy-start.1
  2.5 0.9 %copy-done.1 = f32[40,1536]{1,0:T(8,128)S(1)} copy-done((f32[40,1536]{1,0:T(8,128)S(1)}, f32[40,1536]{1,0:T(8,128)}, u32[]{:S(2)}) %copy-start.1) | copy-done | bytes 245784
  3.5 0.0 copy-start.2
  3.5 0.9 %copy-done.2 = f32[40,1536]{1,0:T(8,128)S(1)} copy-done((f32[40,1536]{1,0:T(8,128)S(1)}, f32[40,1536]{1,0:T(8,128)}, u32[]{:S(2)}) %copy-start.2) | copy-done | bytes 245784
  4.4 0.0 copy-start.3
  4.4 0.9 %copy-done.3 = f32[80,256]{1,0:T(8,128)S(1)} copy-done((f32[80,256]{1,0:T(8,128)S(1)}, f32[80,256]{1,0:T(8,128)}, u32[]{:S(2)}) %copy-start.3) | copy-done | bytes 81944
  5.3 67.1 %tracer_step.1 = f32[8,80,256]{2,1,0:T(8,128)S(1)} custom-call(f32[8,80,256]{2,1,0:T(8,128)S(1)} %copy-done, s32[1,256]{1,0:T(1,128)S(1)} %bitcast.1, s32[6,256]{1,0:T(8,128)S(1)} %copy-done.4, s32[2,128]{1,0:T(2,128)S(1)} %copy-done.7, f32[40,1536]{1,0:T(8,128)S(1)} %copy-done.1, f32[40,1536]{1,0:T(8,128)S(1)} %copy-done.2, ...), custom_call_target="tpu_custom_call" | custom-call | tf_op jit(solution)/shard_map/tracer_step/pallas_call | solution.py:365
  72.4 0.8 %copy.13 = f32[8,80,256]{2,1,0:T(8,128)} copy(f32[8,80,256]{2,1,0:T(8,128)S(1)} %tracer_step.1) | data formatting | bytes 1310720
  (1 shorter events, 0.0 us)
Async XLA Ops:
  0.0 0.7 %copy-start.9 = (s32[1536]{0:T(1024)S(1)}, s32[1536]{0:T(1024)}, u32[]{:S(2)}) copy-start(s32[1536]{0:T(1024)} %param.18) | copy-start | bytes 18436
  0.0 0.8 %copy-start.5 = (f32[16,16]{1,0:T(8,128)S(1)}, f32[16,16]{1,0:T(8,128)}, u32[]{:S(2)}) copy-start(f32[16,16]{1,0:T(8,128)} %st_ref.1) | copy-start | bytes 3076
  0.7 0.7 copy-start.4
  0.7 0.7 copy-start.6
  0.8 0.7 copy-start.7
  0.8 0.7 copy-start.8
  1.5 1.1 %copy-start = (f32[8,80,256]{2,1,0:T(8,128)S(1)}, f32[8,80,256]{2,1,0:T(8,128)}, u32[]{:S(2)}) copy-start(f32[8,80,256]{2,1,0:T(8,128)} %tr_ref.1) | copy-start | bytes 1966084
  2.5 0.9 %copy-start.1 = (f32[40,1536]{1,0:T(8,128)S(1)}, f32[40,1536]{1,0:T(8,128)}, u32[]{:S(2)}) copy-start(f32[40,1536]{1,0:T(8,128)} %tp_ref.1) | copy-start | bytes 737284
  3.5 0.9 %copy-start.2 = (f32[40,1536]{1,0:T(8,128)S(1)}, f32[40,1536]{1,0:T(8,128)}, u32[]{:S(2)}) copy-start(f32[40,1536]{1,0:T(8,128)} %ed_ref.1) | copy-start | bytes 737284
  4.4 0.9 %copy-start.3 = (f32[80,256]{1,0:T(8,128)S(1)}, f32[80,256]{1,0:T(8,128)}, u32[]{:S(2)}) copy-start(f32[80,256]{1,0:T(8,128)} %vd_ref.1) | copy-start | bytes 245764

commit v2 on v1

--- a/solution.py
+++ b/solution.py
@@ -15,12 +15,15 @@
 NT_DIMS = (((1,), (1,)), ((), ()))
 
 
-def steps(count, fn):
+LANES = 128
+
+
+def steps(count, fn, start=0):
     if count <= 8:
-        for i in range(count):
+        for i in range(start, count):
             fn(i)
     else:
-        lax.fori_loop(0, count, lambda i, c: (fn(i), c)[1], 0)
+        lax.fori_loop(start, count, lambda i, c: (fn(i), c)[1], 0)
 
 
 def dot(a, b):
@@ -113,10 +116,19 @@
 
     place = lax.broadcasted_iota(jnp.int32, (cap, recs), 0)
 
-    def pack(block):
+    pieces = cap // LANES
+    slot_row = lax.broadcasted_iota(jnp.int32, (8, LANES), 0)
+
+    def pack(block, ref):
         sel = onehot(place == target - block * cap)
         both = dot_nt(rec_a[...], sel)
-        return both[:width] + both[width:]
+        got = both[:width] + both[width:]
+        tile = jnp.zeros((8, LANES), F32)
+        for i in range(pieces):
+            piece = slice(i * LANES, (i + 1) * LANES)
+            ref[block, i * layers:(i + 1) * layers, :] = got[:layers, piece]
+            tile = jnp.where(slot_row == i, got[layers:layers + 8, piece], tile)
+        ref[block, pieces * layers:pieces * layers + 8, :] = tile
 
     def rec_copy(block, source):
         return pltpu.make_async_remote_copy(
@@ -132,22 +144,18 @@
 
     def ship(i):
         block = partner(offset(i))
-        send[block] = pack(block)
+        pack(block, send)
         rec_copy(block, me).start()
 
-    steps(blocks - 1, ship)
-    arrived[me] = pack(me)
+    early = 3 if blocks == 8 else 0
+    for i in range(early):
+        ship(i)
 
     local_rows = lax.broadcasted_iota(jnp.int32, (cells, cols), 0)
     for side in range(2):
         sel = onehot(local_rows == halo_ref[side:side + 1, :])
         hsel[0:cells, side * cols:(side + 1) * cols] = sel
         hsel[cells:2 * cells, side * cols:(side + 1) * cols] = sel
-    ext_rows = lax.broadcasted_iota(jnp.int32, (ext, cells), 0)
-    for k in range(6):
-        sel = onehot(ext_rows == nb_ref[k:k + 1, :])
-        gsel[k, 0:ext, :] = sel
-        gsel[k, ext:2 * ext, :] = sel
 
     field[pl.ds(sub * own, own)] = tr_ref[:, pl.ds(mine, half), :]
     tr_copy.wait()
@@ -176,6 +184,41 @@
     rims = rim_copies(rim_out, rim_in, rim_send, rim_recv)
     for copy in rims:
         copy.start()
+
+    steps(blocks - 1, ship, early)
+    pack(me, arrived)
+
+    ext_rows = lax.broadcasted_iota(jnp.int32, (ext, cells), 0)
+    for k in range(6):
+        sel = onehot(ext_rows == nb_ref[k:k + 1, :])
+        gsel[k, 0:ext, :] = sel
+        gsel[k, ext:2 * ext, :] = sel
+
+    flow[...] = jnp.zeros_like(flow)
+    slot_id = lax.broadcasted_iota(jnp.int32, (slots, cap), 0).astype(F32) + 1.0
+
+    def unpack(block):
+        tile = arrived[block, pieces * layers:pieces * layers + 8, :]
+        label = jnp.concatenate([tile[i:i + 1] for i in range(pieces)], axis=1)
+        sel = onehot(slot_id == label)
+        value = jnp.concatenate(
+            [arrived[block, i * layers:(i + 1) * layers, :] for i in range(pieces)], axis=1
+        )
+        top = value.astype(BF16).astype(F32)
+        both = dot_nt(jnp.concatenate([top, value - top], axis=0).astype(BF16), sel)
+        flow[...] += both[:layers] + both[layers:]
+
+    unpack(me)
+
+    def take(i):
+        block = partner(blocks - offset(i))
+        rec_copy(block, block).wait_recv()
+        unpack(block)
+
+    before_rims = 2 if blocks == 8 else 0
+    for i in range(before_rims):
+        take(i)
+
     for copy in rims:
         copy.wait_recv()
 
@@ -195,25 +238,7 @@
         far_count = dot(count_ext, gsel[k, 0:ext])[0:1]
         masks[k] = jnp.where(layer_f < far_count, wet, 0.0)
 
-    flow[...] = jnp.zeros_like(flow)
-    slot_id = lax.broadcasted_iota(jnp.int32, (slots, cap), 0).astype(F32) + 1.0
-
-    def unpack(block):
-        got = arrived[block]
-        sel = onehot(slot_id == got[width - 8:width - 7, :])
-        body = got[:width - 8]
-        top = body.astype(BF16).astype(F32)
-        both = dot_nt(jnp.concatenate([top, body - top], axis=0).astype(BF16), sel)
-        flow[...] += both[:width - 8] + both[width - 8:]
-
-    unpack(me)
-
-    def take(i):
-        block = partner(blocks - offset(i))
-        rec_copy(block, block).wait_recv()
-        unpack(block)
-
-    steps(blocks - 1, take)
+    steps(blocks - 1, take, before_rims)
 
     total = jnp.zeros((half, cells), F32)
     for k in range(6):
@@ -240,26 +265,23 @@
         lim[here, :] = spread / (spread + size + LIMIT_PAD)
         return c
 
-    lax.fori_loop(0, tracers, limiter, 0)
-
-    hi, lo = split(lim[...])
-    la[:, 0:cells] = hi
-    la[:, ext:ext + cells] = lo
-    picked = dot(hi, hsel[0:cells]) + dot(lo, hsel[cells:2 * cells])
-    for side in range(2):
-        lrim_out[side] = picked[:, side * cols:(side + 1) * cols]
-    lrims = rim_copies(lrim_out, lrim_in, lrim_send, lrim_recv)
-    for copy in lrims:
-        copy.start()
-    for copy in lrims:
-        copy.wait_recv()
-    for side in range(2):
-        hi, lo = split(lrim_in[side])
-        first = cells + side * cols
-        la[:, first:first + cols] = hi
-        la[:, ext + first:ext + first + cols] = lo
-    for k in range(6):
-        lk[k] = dot(la[...], gsel[k])
+    groups = lrim_out.shape[0]
+    each = tracers // groups
+    chunk_rows = each * half
+    lrims = []
+    for g in range(groups):
+        part = slice(g * chunk_rows, (g + 1) * chunk_rows)
+        lax.fori_loop(g * each, (g + 1) * each, limiter, 0)
+        hi, lo = split(lim[part])
+        la[part, 0:cells] = hi
+        la[part, ext:ext + cells] = lo
+        picked = dot(hi, hsel[0:cells]) + dot(lo, hsel[cells:2 * cells])
+        for side in range(2):
+            lrim_out[g, side] = picked[:, side * cols:(side + 1) * cols]
+        copies = rim_copies(lrim_out.at[g], lrim_in.at[g], lrim_send.at[g], lrim_recv.at[g])
+        for copy in copies:
+            copy.start()
+        lrims.append(copies)
 
     def advect(t, c):
         q = field[t]
@@ -272,22 +294,28 @@
         adv[t] = q - net
         return c
 
-    lax.fori_loop(0, tracers, advect, 0)
-
-    @pl.when(sub == 0)
-    def _():
-        edge_out[...] = adv[:, half - 1, :]
-
-    @pl.when(sub == 1)
-    def _():
-        edge_out[...] = adv[:, 0, :]
-
-    edge_copy = pltpu.make_async_remote_copy(
-        src_ref=edge_out, dst_ref=edge_in, send_sem=edge_sem.at[0], recv_sem=edge_sem.at[1],
-        device_id=other, device_id_type=MESH,
-    )
-    edge_copy.start()
-    edge_copy.wait()
+    edge_copies = []
+    for g in range(groups):
+        part = slice(g * chunk_rows, (g + 1) * chunk_rows)
+        for copy in lrims[g]:
+            copy.wait_recv()
+        for side in range(2):
+            hi, lo = split(lrim_in[g, side])
+            first = cells + side * cols
+            la[part, first:first + cols] = hi
+            la[part, ext + first:ext + first + cols] = lo
+        for k in range(6):
+            lk[k, part] = dot(la[part], gsel[k])
+        lax.fori_loop(g * each, (g + 1) * each, advect, 0)
+        group = slice(g * each, (g + 1) * each)
+        edge_out[g] = jnp.where(sub == 0, adv[group, half - 1, :], adv[group, 0, :])
+        edge_copy = pltpu.make_async_remote_copy(
+            src_ref=edge_out.at[g], dst_ref=edge_in.at[g],
+            send_sem=edge_sem.at[g, 0], recv_sem=edge_sem.at[g, 1],
+            device_id=other, device_id_type=MESH,
+        )
+        edge_copy.start()
+        edge_copies.append(edge_copy)
 
     counts = lc_ref[...]
     upper = vd_ref[pl.ds(mine, half), :]
@@ -299,18 +327,21 @@
     w_up = jnp.where(row == 0, jnp.where(sub == 0, 0.0, cut), pltpu.roll(w_down, 1, 0))
     light = REACT_RATE * jnp.exp(-3.0 * layer_f / layers) * wet
 
-    def mix(t, c):
+    def mix(g, i):
+        t = g * each + i
         a = adv[t]
-        across = edge_in[pl.ds(t, 1), :]
+        across = edge_in[g, pl.ds(i, 1), :]
         below = jnp.where(row == half - 1, across, pltpu.roll(a, half - 1, 0))
         above = jnp.where(row == 0, across, pltpu.roll(a, 1, 0))
         m = a + w_down * (below - a) - w_up * (a - above)
         adv[t] = m
         sq = m * m
         field[t] = sq / (hs_ref[t] + sq)
-        return c
-
-    lax.fori_loop(0, tracers, mix, 0)
+
+    for g in range(groups):
+        edge_copies[g].wait()
+        for i in range(each):
+            mix(g, i)
 
     def react(t):
         acc = st_ref[t, 0] * field[0]
@@ -340,7 +371,7 @@
         rec_copy(partner(i + 1), me).wait_send()
 
     steps(blocks - 1, drain)
-    for copy in rims + lrims:
+    for copy in sum(lrims, rims):
         copy.wait_send()
 
 
@@ -358,10 +389,13 @@
     n_role = lax.axis_size("role")
     blocks = lax.axis_size("cells") * n_role
     cap = -(-(2 * recs // blocks) // 128) * 128
+    packed = cap // LANES * layers + 8
     width = layers + 8
+    groups = 4
     vmem = pl.BlockSpec(memory_space=pltpu.VMEM)
     smem = pl.BlockSpec(memory_space=pltpu.SMEM)
     pair = pltpu.SemaphoreType.DMA((2,))
+    fours = pltpu.SemaphoreType.DMA((groups, 2))
     return pl.pallas_call(
         functools.partial(kernel, blocks, n_role, cap),
         out_shape=jax.ShapeDtypeStruct(tracers.shape, F32),
@@ -370,8 +404,8 @@
         scratch_shapes=[
             pltpu.VMEM((count, half, cells), F32),
             pltpu.VMEM((2 * width, recs), BF16),
-            pltpu.VMEM((blocks, width, cap), F32),
-            pltpu.VMEM((blocks, width, cap), F32),
+            pltpu.VMEM((blocks, packed, LANES), F32),
+            pltpu.VMEM((blocks, packed, LANES), F32),
             pltpu.VMEM((layers, 6 * cells), F32),
             pltpu.VMEM((rows, 2 * ext), BF16),
             pltpu.VMEM((rows, 2 * ext), BF16),
@@ -381,18 +415,18 @@
             pltpu.VMEM((6, rows, cells), F32),
             pltpu.VMEM((rows, cells), F32),
             pltpu.VMEM((count, half, cells), F32),
-            pltpu.VMEM((count, cells), F32),
-            pltpu.VMEM((count, cells), F32),
+            pltpu.VMEM((groups, count // groups, cells), F32),
+            pltpu.VMEM((groups, count // groups, cells), F32),
             pltpu.VMEM((2, rows + 8, cols), F32),
             pltpu.VMEM((2, rows + 8, cols), F32),
-            pltpu.VMEM((2, rows, cols), F32),
-            pltpu.VMEM((2, rows, cols), F32),
+            pltpu.VMEM((groups, 2, rows // groups, cols), F32),
+            pltpu.VMEM((groups, 2, rows // groups, cols), F32),
             pltpu.VMEM((own, half, cells), F32),
             pltpu.VMEM((6, half, cells), F32),
             pltpu.VMEM((13, half, cells), F32),
             pltpu.SemaphoreType.DMA((blocks,)),
             pltpu.SemaphoreType.DMA((blocks,)),
-            pair, pair, pair, pair, pair, pair, pair,
+            pair, pair, pair, fours, fours, fours, pair,
         ],
         compiler_params=pltpu.CompilerParams(
             collective_id=0, has_side_effects=True, vmem_limit_bytes=52 * 1024 * 1024

time: 73.6 us -> 64.2 us (0.87)
  Pallas kernels: 67.1 us -> 57.7 us
    pallas_call x1, Pallas kernels: 67.1 us -> 57.7 us  [body(): pl.pallas_call(functools.partial(kernel, blocks, n_role, cap), out_shape=...]
where the time goes in v2:
time: 64.2 us; the launch traced here: 63.9 us
  Pallas kernels  57.7 us (90%)
  local copies, waits for them, and re-layouts  6.1 us (10%)
    pallas_call x1, Pallas kernels, body(): pl.pallas_call(functools.partial(kernel, blocks, n_role, cap), out_shape=...  57.7 us
    unnamed x21, local copies, waits for them, and re-layouts  5.37 us

profile of v2, /device:TPU:0, one launch (start us, length us, event | category | flops | bytes accessed | tf_op | source)
XLA Modules:
  0.0 63.9 jit_solution(12572049190569022082)
XLA Ops:
  0.0 0.0 copy-start.9
  0.0 0.0 copy-start.5
  0.0 0.7 %reshape.10.dest_ref = s32[1,1536]{1,0:T(1,128)S(1)} reshape(s32[1536]{0:T(1024)} %param.17) | data formatting | bytes 12288 | tf_op jit(solution)/shard_map/reshape | solution.py:437
  0.7 0.0 copy-done.9
  0.7 0.0 copy-start.4
  0.7 0.0 copy-start.6
  0.8 0.0 copy-start.7
  0.8 0.0 copy-start.8
  0.8 0.0 copy-done.5
  0.8 0.6 copy-done.4
  1.4 0.0 copy-done.6
  1.4 0.0 copy-done.7
  1.4 0.0 copy-done.8
  1.5 0.0 copy-start
  1.5 1.1 %copy-done = f32[8,80,256]{2,1,0:T(8,128)S(1)} copy-done((f32[8,80,256]{2,1,0:T(8,128)S(1)}, f32[8,80,256]{2,1,0:T(8,128)}, u32[]{:S(2)}) %copy-start) | copy-done | bytes 655384
  2.5 0.0 copy-start.1
  2.5 0.9 %copy-done.1 = f32[40,1536]{1,0:T(8,128)S(1)} copy-done((f32[40,1536]{1,0:T(8,128)S(1)}, f32[40,1536]{1,0:T(8,128)}, u32[]{:S(2)}) %copy-start.1) | copy-done | bytes 245784
  3.5 0.0 copy-start.2
  3.5 0.9 %copy-done.2 = f32[40,1536]{1,0:T(8,128)S(1)} copy-done((f32[40,1536]{1,0:T(8,128)S(1)}, f32[40,1536]{1,0:T(8,128)}, u32[]{:S(2)}) %copy-start.2) | copy-done | bytes 245784
  4.4 0.0 copy-start.3
  4.4 0.9 %copy-done.3 = f32[80,256]{1,0:T(8,128)S(1)} copy-done((f32[80,256]{1,0:T(8,128)S(1)}, f32[80,256]{1,0:T(8,128)}, u32[]{:S(2)}) %copy-start.3) | copy-done | bytes 81944
  5.3 57.7 %tracer_step.1 = f32[8,80,256]{2,1,0:T(8,128)S(1)} custom-call(f32[8,80,256]{2,1,0:T(8,128)S(1)} %copy-done, s32[1,256]{1,0:T(1,128)S(1)} %bitcast.1, s32[6,256]{1,0:T(8,128)S(1)} %copy-done.4, s32[2,128]{1,0:T(2,128)S(1)} %copy-done.7, f32[40,1536]{1,0:T(8,128)S(1)} %copy-done.1, f32[40,1536]{1,0:T(8,128)S(1)} %copy-done.2, ...), custom_call_target="tpu_custom_call" | custom-call | tf_op jit(solution)/shard_map/tracer_step/pallas_call | solution.py:399
  63.1 0.8 %copy.13 = f32[8,80,256]{2,1,0:T(8,128)} copy(f32[8,80,256]{2,1,0:T(8,128)S(1)} %tracer_step.1) | data formatting | bytes 1310720
  (1 shorter events, 0.0 us)
Async XLA Ops:
  0.0 0.7 %copy-start.9 = (s32[1536]{0:T(1024)S(1)}, s32[1536]{0:T(1024)}, u32[]{:S(2)}) copy-start(s32[1536]{0:T(1024)} %param.18) | copy-start | bytes 18436
  0.0 0.8 %copy-start.5 = (f32[16,16]{1,0:T(8,128)S(1)}, f32[16,16]{1,0:T(8,128)}, u32[]{:S(2)}) copy-start(f32[16,16]{1,0:T(8,128)} %st_ref.1) | copy-start | bytes 3076
  0.7 0.7 %copy-start.4 = (s32[6,256]{1,0:T(8,128)S(1)}, s32[6,256]{1,0:T(8,128)}, u32[]{:S(2)}) copy-start(s32[6,256]{1,0:T(8,128)} %nb_ref.1) | copy-start | bytes 18436
  0.7 0.7 %copy-start.6 = (s32[256]{0:T(256)S(1)}, s32[256]{0:T(256)}, u32[]{:S(2)}) copy-start(s32[256]{0:T(256)} %param.12) | copy-start | bytes 3076
  0.8 0.7 %copy-start.7 = (s32[2,128]{1,0:T(2,128)S(1)}, s32[2,128]{1,0:T(2,128)}, u32[]{:S(2)}) copy-start(s32[2,128]{1,0:T(2,128)} %halo_ref.1) | copy-start | bytes 3076
  0.8 0.7 %copy-start.8 = (f32[16]{0:T(128)S(1)}, f32[16]{0:T(128)}, u32[]{:S(2)}) copy-start(f32[16]{0:T(128)} %hs_ref.1) | copy-start | bytes 196
  1.5 1.1 %copy-start = (f32[8,80,256]{2,1,0:T(8,128)S(1)}, f32[8,80,256]{2,1,0:T(8,128)}, u32[]{:S(2)}) copy-start(f32[8,80,256]{2,1,0:T(8,128)} %tr_ref.1) | copy-start | bytes 1966084
  2.5 0.9 %copy-start.1 = (f32[40,1536]{1,0:T(8,128)S(1)}, f32[40,1536]{1,0:T(8,128)}, u32[]{:S(2)}) copy-start(f32[40,1536]{1,0:T(8,128)} %tp_ref.1) | copy-start | bytes 737284
  3.5 0.9 %copy-start.2 = (f32[40,1536]{1,0:T(8,128)S(1)}, f32[40,1536]{1,0:T(8,128)}, u32[]{:S(2)}) copy-start(f32[40,1536]{1,0:T(8,128)} %ed_ref.1) | copy-start | bytes 737284
  4.4 0.9 %copy-start.3 = (f32[80,256]{1,0:T(8,128)S(1)}, f32[80,256]{1,0:T(8,128)}, u32[]{:S(2)}) copy-start(f32[80,256]{1,0:T(8,128)} %vd_ref.1) | copy-start | bytes 245764

commit v3 on v2

--- a/solution.py
+++ b/solution.py
@@ -77,7 +77,6 @@
 
     steps(blocks - 1, greet)
     pl.semaphore_signal(barrier, inc=1, device_id=other, device_id_type=MESH)
-    pl.semaphore_wait(barrier, blocks)
 
     mine = pl.multiple_of(sub * half, half)
     theirs = pl.multiple_of((1 - sub) * half, half)
@@ -88,7 +87,6 @@
         send_sem=tr_sem.at[0], recv_sem=tr_sem.at[1],
         device_id=other, device_id_type=MESH,
     )
-    tr_copy.start()
 
     dest = dest_ref[...]
     block_id = lax.broadcasted_iota(jnp.int32, (max(blocks, 8), recs), 0)
@@ -113,6 +111,9 @@
     width = payload.shape[0]
     top = payload.astype(BF16).astype(F32)
     rec_a[...] = jnp.concatenate([top, payload - top], axis=0).astype(BF16)
+
+    pl.semaphore_wait(barrier, blocks)
+    tr_copy.start()
 
     place = lax.broadcasted_iota(jnp.int32, (cap, recs), 0)
 

time: 64.2 us -> 64.4 us (level)
  no operation moved by 1% of the time
where the time goes in v3:
time: 64.4 us; the launch traced here: 64.1 us
  Pallas kernels  57.9 us (90%)
  local copies, waits for them, and re-layouts  6.1 us (9%)
    pallas_call x1, Pallas kernels, body(): pl.pallas_call(functools.partial(kernel, blocks, n_role, cap), out_shape=...  57.9 us
    unnamed x21, local copies, waits for them, and re-layouts  5.37 us

profile of v3, /device:TPU:0, one launch (start us, length us, event | category | flops | bytes accessed | tf_op | source)
XLA Modules:
  0.0 64.1 jit_solution(6502997493855994897)
XLA Ops:
  0.0 0.0 copy-start.9
  0.0 0.0 copy-start.5
  0.0 0.7 %reshape.10.dest_ref = s32[1,1536]{1,0:T(1,128)S(1)} reshape(s32[1536]{0:T(1024)} %param.17) | data formatting | bytes 12288 | tf_op jit(solution)/shard_map/reshape | solution.py:438
  0.7 0.0 copy-done.9
  0.7 0.0 copy-start.4
  0.7 0.0 copy-start.6
  0.8 0.0 copy-start.7
  0.8 0.0 copy-start.8
  0.8 0.0 copy-done.5
  0.8 0.6 copy-done.4
  1.4 0.0 copy-done.6
  1.4 0.0 copy-done.7
  1.4 0.0 copy-done.8
  1.5 0.0 copy-start
  1.5 1.1 %copy-done = f32[8,80,256]{2,1,0:T(8,128)S(1)} copy-done((f32[8,80,256]{2,1,0:T(8,128)S(1)}, f32[8,80,256]{2,1,0:T(8,128)}, u32[]{:S(2)}) %copy-start) | copy-done | bytes 655384
  2.5 0.0 copy-start.1
  2.5 0.9 %copy-done.1 = f32[40,1536]{1,0:T(8,128)S(1)} copy-done((f32[40,1536]{1,0:T(8,128)S(1)}, f32[40,1536]{1,0:T(8,128)}, u32[]{:S(2)}) %copy-start.1) | copy-done | bytes 245784
  3.5 0.0 copy-start.2
  3.5 0.9 %copy-done.2 = f32[40,1536]{1,0:T(8,128)S(1)} copy-done((f32[40,1536]{1,0:T(8,128)S(1)}, f32[40,1536]{1,0:T(8,128)}, u32[]{:S(2)}) %copy-start.2) | copy-done | bytes 245784
  4.4 0.0 copy-start.3
  4.4 0.9 %copy-done.3 = f32[80,256]{1,0:T(8,128)S(1)} copy-done((f32[80,256]{1,0:T(8,128)S(1)}, f32[80,256]{1,0:T(8,128)}, u32[]{:S(2)}) %copy-start.3) | copy-done | bytes 81944
  5.3 57.9 %tracer_step.1 = f32[8,80,256]{2,1,0:T(8,128)S(1)} custom-call(f32[8,80,256]{2,1,0:T(8,128)S(1)} %copy-done, s32[1,256]{1,0:T(1,128)S(1)} %bitcast.1, s32[6,256]{1,0:T(8,128)S(1)} %copy-done.4, s32[2,128]{1,0:T(2,128)S(1)} %copy-done.7, f32[40,1536]{1,0:T(8,128)S(1)} %copy-done.1, f32[40,1536]{1,0:T(8,128)S(1)} %copy-done.2, ...), custom_call_target="tpu_custom_call" | custom-call | tf_op jit(solution)/shard_map/tracer_step/pallas_call | solution.py:400
  63.2 0.8 %copy.13 = f32[8,80,256]{2,1,0:T(8,128)} copy(f32[8,80,256]{2,1,0:T(8,128)S(1)} %tracer_step.1) | data formatting | bytes 1310720
  (1 shorter events, 0.0 us)
Async XLA Ops:
  0.0 0.7 %copy-start.9 = (s32[1536]{0:T(1024)S(1)}, s32[1536]{0:T(1024)}, u32[]{:S(2)}) copy-start(s32[1536]{0:T(1024)} %param.18) | copy-start | bytes 18436
  0.0 0.8 %copy-start.5 = (f32[16,16]{1,0:T(8,128)S(1)}, f32[16,16]{1,0:T(8,128)}, u32[]{:S(2)}) copy-start(f32[16,16]{1,0:T(8,128)} %st_ref.1) | copy-start | bytes 3076
  0.7 0.7 %copy-start.4 = (s32[6,256]{1,0:T(8,128)S(1)}, s32[6,256]{1,0:T(8,128)}, u32[]{:S(2)}) copy-start(s32[6,256]{1,0:T(8,128)} %nb_ref.1) | copy-start | bytes 18436
  0.7 0.7 %copy-start.6 = (s32[256]{0:T(256)S(1)}, s32[256]{0:T(256)}, u32[]{:S(2)}) copy-start(s32[256]{0:T(256)} %param.12) | copy-start | bytes 3076
  0.8 0.7 %copy-start.7 = (s32[2,128]{1,0:T(2,128)S(1)}, s32[2,128]{1,0:T(2,128)}, u32[]{:S(2)}) copy-start(s32[2,128]{1,0:T(2,128)} %halo_ref.1) | copy-start | bytes 3076
  0.8 0.7 %copy-start.8 = (f32[16]{0:T(128)S(1)}, f32[16]{0:T(128)}, u32[]{:S(2)}) copy-start(f32[16]{0:T(128)} %hs_ref.1) | copy-start | bytes 196
  1.5 1.1 %copy-start = (f32[8,80,256]{2,1,0:T(8,128)S(1)}, f32[8,80,256]{2,1,0:T(8,128)}, u32[]{:S(2)}) copy-start(f32[8,80,256]{2,1,0:T(8,128)} %tr_ref.1) | copy-start | bytes 1966084
  2.5 0.9 %copy-start.1 = (f32[40,1536]{1,0:T(8,128)S(1)}, f32[40,1536]{1,0:T(8,128)}, u32[]{:S(2)}) copy-start(f32[40,1536]{1,0:T(8,128)} %tp_ref.1) | copy-start | bytes 737284
  3.5 0.9 %copy-start.2 = (f32[40,1536]{1,0:T(8,128)S(1)}, f32[40,1536]{1,0:T(8,128)}, u32[]{:S(2)}) copy-start(f32[40,1536]{1,0:T(8,128)} %ed_ref.1) | copy-start | bytes 737284
  4.4 0.9 %copy-start.3 = (f32[80,256]{1,0:T(8,128)S(1)}, f32[80,256]{1,0:T(8,128)}, u32[]{:S(2)}) copy-start(f32[80,256]{1,0:T(8,128)} %vd_ref.1) | copy-start | bytes 245764
